TPU v7x, 32 devices: a whole 2x2x4 slice. The times are simulated.
32 devices in a mesh: dp: 4 (over y, core), expert: 8 (over z, x).
Axes of the slice: x: 2, y: 2, z: 4, core: 2. Of those that a mesh axis runs over, the one named last changes fastest.
Arguments:
- tokens: bfloat16 [6144, 4096], P(('dp', 'expert')), may hold values from -6 to 6
- cotangent: bfloat16 [6144, 4096], P(('dp', 'expert')), may hold values from -6 to 6
- expert_ids: int32 [6144, 6], P(('dp', 'expert')), may hold values from 0 to 63, as said below
- route_weights: float32 [6144, 6], P(('dp', 'expert')), may hold values from 0.05 to 1
- expert_weights: bfloat16 [8, 704, 3, 4096], P('expert'), may hold values from -0.09375 to 0.09375
Outputs:
- input_grad: bfloat16 [6144, 4096], P(('dp', 'expert'))
- route_grad: bfloat16 [6144, 6], P(('dp', 'expert'))
- weight_grad: float32 [8, 704, 3, 4096], P('expert', 'dp')
Inputs may be any that keep to these rules, and one draw needn't show every extreme that they name: `expert_ids`: each row names 6 different experts. Only experts below 8 are in this window; in the rows of one device (aligned blocks of 192 rows) each of them is named at most 36 times.
All inputs are finite; a program needn't handle non-finite values.
Results may differ from a plain program's by a relative error of at most 0.015.
Values may be sent and summed in bfloat16 or wider, within the bound.
A program may use at most 128 MiB of HBM per device.

v0:
```python
import jax
import jax.numpy as jnp
from jax import lax
from jax.sharding import PartitionSpec as P

CAP = 36


def shards(tokens, cotangent, expert_ids, route_weights, expert_weights):
    experts_here = lax.axis_size("expert")
    tok_rows, model_width = tokens.shape
    top_count = expert_ids.shape[1]
    flat_ids = expert_ids.reshape(-1)
    route_count = flat_ids.shape[0]
    total_slots = experts_here * CAP
    columns = jnp.arange(experts_here, dtype=jnp.int32)
    onehot = (flat_ids[:, None] == columns[None, :]).astype(jnp.int32)
    running = jnp.cumsum(onehot, axis=0) - 1
    slot_index = jnp.sum(onehot * running, axis=1)
    is_live = flat_ids < experts_here
    target = jnp.where(is_live, flat_ids * CAP + slot_index, total_slots)
    source = (
        jnp.full((total_slots,), route_count, jnp.int32)
        .at[target]
        .set(jnp.arange(route_count, dtype=jnp.int32), mode="drop")
    )
    filled = source < route_count
    source_safe = jnp.minimum(source, route_count - 1)
    owner_row = source_safe // top_count
    picker = (
        (owner_row[:, None] == jnp.arange(tok_rows, dtype=jnp.int32)[None, :]) & filled[:, None]
    ).astype(jnp.bfloat16)
    send_inputs = (
        jnp.dot(picker, tokens, preferred_element_type=jnp.float32)
        .astype(jnp.bfloat16)
        .reshape(experts_here, CAP, model_width)
    )
    send_cot = (
        jnp.dot(picker, cotangent, preferred_element_type=jnp.float32)
        .astype(jnp.bfloat16)
        .reshape(experts_here, CAP, model_width)
    )
    send_scale = (
        jnp.where(filled, route_weights.reshape(-1)[source_safe], jnp.float32(0.0))
        .astype(jnp.bfloat16)
        .reshape(experts_here, CAP)
    )
    weights = expert_weights[0]
    gate_up_rows = weights[:, :2, :]
    recv_inputs, recv_cot, recv_scale = (
        lax.all_to_all(send_inputs, "expert", split_axis=0, concat_axis=0, tiled=True),
        lax.all_to_all(send_cot, "expert", split_axis=0, concat_axis=0, tiled=True),
        lax.all_to_all(send_scale, "expert", split_axis=0, concat_axis=0, tiled=True),
    )
    token_rows = recv_inputs.reshape(-1, model_width)
    pre_acts = jnp.einsum(
        "md,hkd->mkh", token_rows, gate_up_rows, preferred_element_type=jnp.float32
    )
    gate_pre = pre_acts[:, 0, :]
    up_pre = pre_acts[:, 1, :]
    logistic = jax.nn.sigmoid(gate_pre)
    recompute_hidden = (gate_pre * logistic * up_pre).astype(jnp.bfloat16)
    gate_pre, up_pre, logistic, hidden = (gate_pre, up_pre, logistic, recompute_hidden)
    cot_rows = recv_cot.reshape(-1, model_width)
    row_scale = recv_scale.reshape(-1).astype(jnp.float32)[:, None]
    back_proj = jnp.einsum(
        "md,hd->mh", cot_rows, weights[:, 2, :], preferred_element_type=jnp.float32
    )
    route_rows = jnp.sum(hidden.astype(jnp.float32) * back_proj, axis=1).astype(jnp.bfloat16)
    scaled = (row_scale * cot_rows.astype(jnp.float32)).astype(jnp.bfloat16)
    grad_hidden = row_scale * back_proj
    gate_delta = (grad_hidden * up_pre * logistic * (1.0 + gate_pre * (1.0 - logistic))).astype(
        jnp.bfloat16
    )
    up_delta = (grad_hidden * gate_pre * logistic).astype(jnp.bfloat16)
    deltas = jnp.stack([gate_delta, up_delta], axis=1)
    input_rows = jnp.einsum(
        "mkh,hkd->md", deltas, gate_up_rows, preferred_element_type=jnp.float32
    ).astype(jnp.bfloat16)
    back_rows = lax.all_to_all(
        input_rows.reshape(experts_here, CAP, model_width),
        "expert",
        split_axis=0,
        concat_axis=0,
        tiled=True,
    )
    back_route = lax.all_to_all(
        route_rows.reshape(experts_here, CAP), "expert", split_axis=0, concat_axis=0, tiled=True
    )
    gate_up_term = jnp.einsum("mkh,md->hkd", deltas, token_rows, preferred_element_type=jnp.float32)
    down_term = jnp.einsum("mh,md->hd", hidden, scaled, preferred_element_type=jnp.float32)
    summed = lax.psum_scatter(
        jnp.concatenate([gate_up_term, down_term[:, None, :]], axis=1).astype(jnp.bfloat16),
        "dp",
        scatter_dimension=0,
        tiled=True,
    ).astype(jnp.float32)
    input_grad = jnp.dot(
        picker.T, back_rows.reshape(-1, model_width), preferred_element_type=jnp.float32
    ).astype(jnp.bfloat16)
    flat_back = back_route.reshape(-1)
    target_safe = jnp.minimum(target, total_slots - 1)
    route_grad = jnp.where(is_live, flat_back[target_safe], jnp.zeros((), jnp.bfloat16)).reshape(
        tok_rows, top_count
    )
    return (input_grad, route_grad, summed[None])


def solution(mesh):
    in_specs = (
        P(("dp", "expert"), None),
        P(("dp", "expert"), None),
        P(("dp", "expert"), None),
        P(("dp", "expert"), None),
        P("expert", None, None, None),
    )
    out_specs = (
        P(("dp", "expert"), None),
        P(("dp", "expert"), None),
        P("expert", "dp", None, None),
    )
    return jax.shard_map(shards, mesh=mesh, in_specs=in_specs, out_specs=out_specs, check_vma=False)
```

profile of v0, /device:TPU:0, one launch (start us, length us, event | category | flops | bytes accessed | tf_op | source)
XLA Modules:
  0.0 347.5 jit_solution(18173788882495825920)
XLA Ops:
  12.5 6.4 %scatter_custom_fusion = s32[288]{0:T(512)S(1)} fusion(s32[1152]{0:T(1024)S(1)} %get-tuple-element.13, s32[1152]{0:T(1024)S(1)} %iota.15, s32[]{:T(128)} %constant.13.clone.1), kind=kCustom, calls=%fused_computation.76 | custom fusion | bytes 1156 | tf_op jit(solution)/shard_map/scatter | solution.py:25
  23.1 7.3 %all-to-all-start = ((bf16[8,1,36]{2,1,0:T(2,128)(2,1)}), bf16[8,1,36]{2,1,0:T(2,128)(2,1)S(1)}, u32[]{:S(2)}, u32[]{:S(2)}) async-start(bf16[8,1,36]{2,1,0:T(2,128)(2,1)} %all_to_all.25), calls=%async_computation | async-start | bytes 8192 | tf_op jit(solution)/shard_map/all_to_all | solution.py:53
  32.6 4.1 %reshape.160 = bf16[8,36,4096]{2,1,0:T(8,128)(2,1)} reshape(bf16[288,4096]{1,0:T(8,128)(2,1)} %convolution_convert_fusion.2) | data formatting | bytes 4718592 | tf_op jit(solution)/shard_map/reshape | solution.py:41
  36.8 6.0 %all-to-all-start.1 = ((bf16[8,36,4096]{2,1,0:T(8,128)(2,1)}), bf16[8,36,4096]{2,1,0:T(8,128)(2,1)S(1)}, u32[]{:S(2)}, u32[]{:S(2)}) async-start(bf16[8,36,4096]{2,1,0:T(8,128)(2,1)} %reshape.160), calls=%async_computation.1 | async-start | bytes 5242880 | tf_op jit(solution)/shard_map/all_to_all | solution.py:52
  42.7 3.7 %convolution_convert_fusion.1 = bf16[288,4096]{1,0:T(8,128)(2,1)} fusion(bf16[192,4096]{1,0:T(8,128)(2,1)} %param.5, s32[288]{0:T(512)S(1)} %get-tuple-element.20, pred[288]{0:T(512)(128)(4,1)S(1)} %get-tuple-element.15), kind=kOutput, calls=%fused_computation.15 | convolution fusion | flops 454275072 | bytes 3933600 | tf_op jit(solution)/shard_map/dot_general | solution.py:34
  46.4 4.1 %reshape.162 = bf16[8,36,4096]{2,1,0:T(8,128)(2,1)} reshape(bf16[288,4096]{1,0:T(8,128)(2,1)} %convolution_convert_fusion.1) | data formatting | bytes 4718592 | tf_op jit(solution)/shard_map/reshape | solution.py:36
  50.5 51.2 %all-to-all-done.1 = bf16[8,36,4096]{2,1,0:T(8,128)(2,1)S(1)} async-done(((bf16[8,36,4096]{2,1,0:T(8,128)(2,1)}), bf16[8,36,4096]{2,1,0:T(8,128)(2,1)S(1)}, u32[]{:S(2)}, u32[]{:S(2)}) %all-to-all-start.1) | async-done | bytes 2359328 | tf_op jit(solution)/shard_map/all_to_all | solution.py:52
  101.6 4.4 %all-to-all-start.2 = ((bf16[8,36,4096]{2,1,0:T(8,128)(2,1)}), bf16[8,36,4096]{2,1,0:T(8,128)(2,1)}, u32[]{:S(2)}, u32[]{:S(2)}) async-start(bf16[8,36,4096]{2,1,0:T(8,128)(2,1)} %reshape.162), calls=%async_computation.2 | async-start | bytes 5242880 | tf_op jit(solution)/shard_map/all_to_all | solution.py:51
  108.7 4.1 %convert_element_type.100 = bf16[288,4096]{1,0:T(8,128)(2,1)} reshape(bf16[8,36,4096]{2,1,0:T(8,128)(2,1)} %multiply_convert_fusion) | data formatting | bytes 4718592 | tf_op jit(solution)/shard_map/convert_element_type | solution.py:70
  112.8 52.3 %all-to-all-done.2 = bf16[8,36,4096]{2,1,0:T(8,128)(2,1)} async-done(((bf16[8,36,4096]{2,1,0:T(8,128)(2,1)}), bf16[8,36,4096]{2,1,0:T(8,128)(2,1)}, u32[]{:S(2)}, u32[]{:S(2)}) %all-to-all-start.2) | async-done | bytes 2359328 | tf_op jit(solution)/shard_map/all_to_all | solution.py:51
  165.0 4.1 %reshape.195 = bf16[288,4096,1]{1,0,2:T(8,128)(2,1)} reshape(bf16[8,36,4096]{2,1,0:T(8,128)(2,1)} %all-to-all-done.2) | data formatting | bytes 4718592 | tf_op jit(solution)/shard_map/reshape | solution.py:55
  169.2 7.6 %fusion.12 = f32[288,2,704]{2,0,1:T(8,128)S(1)} fusion(bf16[288,4096,1]{1,0,2:T(8,128)(2,1)} %reshape.195, bf16[704,3,4096]{2,0,1:T(8,128)(2,1)} %bitcast.101), kind=kOutput, calls=%fused_computation.20 | convolution fusion | flops 3321888768 | bytes 15515648 | tf_op jit(solution)/shard_map/md,hkd->mkh/dot_general | solution.py:56
  178.1 5.1 %fusion.4 = bf16[704,1,4096]{2,0,1:T(8,128)(2,1)} fusion(bf16[288,4096]{1,0:T(8,128)(2,1)S(1)} %copy-done.3, f32[288,2,704]{2,0,1:T(8,128)S(1)} %fusion.12), kind=kOutput, calls=%fused_computation.10 | convolution fusion | flops 1665044480 | bytes 9748480 | tf_op jit(solution)/shard_map/mh,md->hd/dot_general | solution.py:91
  185.2 6.4 %fusion.28 = (bf16[288,1,704]{2,0,1:T(8,128)(2,1)S(1)}, bf16[288,1,704]{2,0,1:T(8,128)(2,1)S(1)}, bf16[288]{0:T(512)(128)(2,1)S(1)}) fusion(f32[288,2,704]{2,0,1:T(8,128)} %copy-done.4, f32[288]{0:T(512)S(1)} %reshape.167, bf16[288,4096]{1,0:T(8,128)(2,1)} %reshape.161, bf16[704,3,4096]{2,0,1:T(8,128)(2,1)} %bitcast.102), kind=kOutput, calls=%fused_computation.42 | convolution fusion | flops 1664999168 | bytes 10708672 | tf_op jit(solution)/shard_map/md,hd->mh/dot_general | solution.py:66
  191.7 6.5 %convert_bitcast_fusion = bf16[704,2,4096]{2,0,1:T(8,128)(2,1)S(1)} fusion(bf16[288,4096,1]{1,0,2:T(8,128)(2,1)S(1)} %copy-done.2, bf16[288,1,704]{2,0,1:T(8,128)(2,1)S(1)} %get-tuple-element.17, bf16[288,1,704]{2,0,1:T(8,128)(2,1)S(1)} %get-tuple-element.16), kind=kOutput, calls=%fused_computation.4 | convolution fusion | flops 3329277952 | bytes 14704640 | tf_op jit(solution)/shard_map/mkh,md->hkd/dot_general | solution.py:90
  198.2 7.0 %pad_maximum_fusion = bf16[704,3,4096]{2,0,1:T(8,128)(2,1)} fusion(bf16[704,1,4096]{2,0,1:T(8,128)(2,1)S(1)} %bitcast.98, bf16[704,2,4096]{2,0,1:T(8,128)(2,1)S(1)} %convert_bitcast_fusion), kind=kLoop, calls=%fused_computation.3 | loop fusion | flops 8650752 | bytes 34603008 | tf_op jit(solution)/shard_map/concatenate | solution.py:93
  205.9 3.6 %all-to-all-start.4 = ((bf16[8,1,36]{2,1,0:T(2,128)(2,1)}), bf16[8,1,36]{2,1,0:T(2,128)(2,1)S(1)}, u32[]{:S(2)}, u32[]{:S(2)}) async-start(bf16[8,1,36]{2,1,0:T(2,128)(2,1)} %convert_element_type.103), calls=%async_computation.4 | async-start | bytes 8192 | tf_op jit(solution)/shard_map/all_to_all | solution.py:87
  209.5 10.0 %fusion.9 = bf16[288,4096]{1,0:T(8,128)(2,1)S(1)} fusion(bf16[704,3,4096]{2,0,1:T(8,128)(2,1)} %bitcast.103, bf16[288,1,704]{2,0,1:T(8,128)(2,1)} %copy-done.5, bf16[288,1,704]{2,0,1:T(8,128)(2,1)S(1)} %get-tuple-element.16), kind=kOutput, calls=%fused_computation.14 | convolution fusion | flops 3323473920 | bytes 14741504 | tf_op jit(solution)/shard_map/mkh,hkd->md/dot_general | solution.py:77
  221.7 6.1 %all-to-all-start.3 = ((bf16[8,36,4096]{2,1,0:T(8,128)(2,1)}), bf16[8,36,4096]{2,1,0:T(8,128)(2,1)S(1)}, u32[]{:S(2)}, u32[]{:S(2)}) async-start(bf16[8,36,4096]{2,1,0:T(8,128)(2,1)} %reshape.164), calls=%async_computation.3 | async-start | bytes 5242880 | tf_op jit(solution)/shard_map/all_to_all | solution.py:80
  227.8 7.3 %gather_fusion.1 = bf16[1152]{0:T(1024)(128)(2,1)S(1)} fusion(bf16[288]{0:T(512)(128)(2,1)S(1)} %reshape.166, s32[2048]{0:T(1024)S(1)} %pad_clamp_fusion), kind=kCustom, calls=%fused_computation.1 | custom fusion | bytes 9216 | tf_op jit(solution)/shard_map/gather | solution.py:103
  236.0 51.2 %all-to-all-done.3 = bf16[8,36,4096]{2,1,0:T(8,128)(2,1)S(1)} async-done(((bf16[8,36,4096]{2,1,0:T(8,128)(2,1)}), bf16[8,36,4096]{2,1,0:T(8,128)(2,1)S(1)}, u32[]{:S(2)}, u32[]{:S(2)}) %all-to-all-start.3) | async-done | bytes 2359328 | tf_op jit(solution)/shard_map/all_to_all | solution.py:80
  289.2 3.9 %convolution_convert_fusion.3 = bf16[192,4096]{1,0:T(8,128)(2,1)} fusion(bf16[288,4096]{1,0:T(8,128)(2,1)} %reshape.165, s32[288]{0:T(512)S(1)} %get-tuple-element.20, pred[288]{0:T(512)(128)(4,1)S(1)} %get-tuple-element.15), kind=kOutput, calls=%fused_computation.18 | convolution fusion | flops 453881856 | bytes 3933600 | tf_op jit(solution)/shard_map/dot_general | solution.py:98
  293.2 40.6 %reduce-scatter.2.cloned.1.call-done = bf16[176,3,4096]{2,0,1:T(8,128)(2,1)} async-done(((bf16[704,3,4096]{2,0,1:T(8,128)(2,1)}), bf16[176,3,4096]{2,0,1:T(8,128)(2,1)}) %reduce-scatter.2.cloned.1.call-update) | async-done | bytes 4325392 | tf_op jit(solution)/shard_map/reduce_scatter | solution.py:92
  333.7 7.0 %bitcast_convert_fusion = f32[1,176,3,4096]{3,1,2,0:T(8,128)} fusion(bf16[176,3,4096]{2,0,1:T(8,128)(2,1)} %reduce-scatter.2.cloned.1.call-done), kind=kLoop, calls=%fused_computation.19 | loop fusion | flops 2162688 | bytes 12976128 | tf_op jit(solution)/shard_map/broadcast_in_dim | solution.py:106
  (59 shorter events, 23.6 us)
Async XLA Ops:
  7.2 23.2 %copy-start = (bf16[192,4096]{1,0:T(8,128)(2,1)S(1)}, bf16[192,4096]{1,0:T(8,128)(2,1)}, u32[]{:S(2)}) copy-start(bf16[192,4096]{1,0:T(8,128)(2,1)} %param.6) | copy-start | bytes 4718596
  23.1 13.6 %all-to-all-start = ((bf16[8,1,36]{2,1,0:T(2,128)(2,1)}), bf16[8,1,36]{2,1,0:T(2,128)(2,1)S(1)}, u32[]{:S(2)}, u32[]{:S(2)}) async-start(bf16[8,1,36]{2,1,0:T(2,128)(2,1)} %all_to_all.25), calls=%async_computation | async-start | bytes 8192 | tf_op jit(solution)/shard_map/all_to_all | solution.py:53
  36.8 64.9 %all-to-all-start.1 = ((bf16[8,36,4096]{2,1,0:T(8,128)(2,1)}), bf16[8,36,4096]{2,1,0:T(8,128)(2,1)S(1)}, u32[]{:S(2)}, u32[]{:S(2)}) async-start(bf16[8,36,4096]{2,1,0:T(8,128)(2,1)} %reshape.160), calls=%async_computation.1 | async-start | bytes 5242880 | tf_op jit(solution)/shard_map/all_to_all | solution.py:52
  101.6 63.4 %all-to-all-start.2 = ((bf16[8,36,4096]{2,1,0:T(8,128)(2,1)}), bf16[8,36,4096]{2,1,0:T(8,128)(2,1)}, u32[]{:S(2)}, u32[]{:S(2)}) async-start(bf16[8,36,4096]{2,1,0:T(8,128)(2,1)} %reshape.162), calls=%async_computation.2 | async-start | bytes 5242880 | tf_op jit(solution)/shard_map/all_to_all | solution.py:51
  106.0 227.7 %reduce-scatter.2.cloned.1.call-start = ((), (), s32[]{:S(2)}) async-start(), calls=%async_computation.6 | async-start | bytes 21626880 | tf_op jit(solution)/shard_map/reduce_scatter | solution.py:92
  169.2 8.9 %copy-start.3 = (bf16[288,4096]{1,0:T(8,128)(2,1)S(1)}, bf16[288,4096]{1,0:T(8,128)(2,1)}, u32[]{:S(2)}) copy-start(bf16[288,4096]{1,0:T(8,128)(2,1)} %convert_element_type.100) | copy-start | bytes 7077892
  176.8 1.3 copy-start.4
  185.2 6.4 %copy-start.2 = (bf16[288,4096,1]{1,0,2:T(8,128)(2,1)S(1)}, bf16[288,4096,1]{1,0,2:T(8,128)(2,1)}, u32[]{:S(2)}) copy-start(bf16[288,4096,1]{1,0,2:T(8,128)(2,1)} %reshape.195) | copy-start | bytes 7077892
  185.2 12.9 %slice-start = ((s8[5767168]{0:T(1024)(128)(4,1)}), s8[4194304]{0:T(1024)(128)(4,1)S(1)}, s32[]{:S(2)}) async-start(s8[5767168]{0:T(1024)(128)(4,1)} %bitcast.97), calls=%async_computation.7 | async-start | bytes 8388608
  191.6 6.5 %copy-start.5 = (bf16[288,1,704]{2,0,1:T(8,128)(2,1)}, bf16[288,1,704]{2,0,1:T(8,128)(2,1)S(1)}, u32[]{:S(2)}) copy-start(bf16[288,1,704]{2,0,1:T(8,128)(2,1)S(1)} %get-tuple-element.17) | copy-start | bytes 1216516
  191.6 6.5 %slice-start.1 = ((s8[5767168]{0:T(1024)(128)(4,1)}), s8[1572864]{0:T(1024)(128)(4,1)S(1)}, s32[]{:S(2)}) async-start(s8[5767168]{0:T(1024)(128)(4,1)} %bitcast.97), calls=%async_computation.8 | async-start | bytes 3145728
  205.9 15.8 %all-to-all-start.4 = ((bf16[8,1,36]{2,1,0:T(2,128)(2,1)}), bf16[8,1,36]{2,1,0:T(2,128)(2,1)S(1)}, u32[]{:S(2)}, u32[]{:S(2)}) async-start(bf16[8,1,36]{2,1,0:T(2,128)(2,1)} %convert_element_type.103), calls=%async_computation.4 | async-start | bytes 8192 | tf_op jit(solution)/shard_map/all_to_all | solution.py:87
  221.7 65.5 %all-to-all-start.3 = ((bf16[8,36,4096]{2,1,0:T(8,128)(2,1)}), bf16[8,36,4096]{2,1,0:T(8,128)(2,1)S(1)}, u32[]{:S(2)}, u32[]{:S(2)}) async-start(bf16[8,36,4096]{2,1,0:T(8,128)(2,1)} %reshape.164), calls=%async_computation.3 | async-start | bytes 5242880 | tf_op jit(solution)/shard_map/all_to_all | solution.py:80
  333.7 7.0 %copy-start.1 = (bf16[192,4096]{1,0:T(8,128)(2,1)S(1)}, bf16[192,4096]{1,0:T(8,128)(2,1)}, u32[]{:S(2)}) copy-start(bf16[192,4096]{1,0:T(8,128)(2,1)} %param.6) | copy-start | bytes 4718596
Sparse Core Ops, SparseCore 0:
  205.3 128.3 reduce-scatter.1
where the time goes:
time: 348 us
  waiting for transfers between devices  195 us (56%)
  local copies, waits for them, and re-layouts  45.5 us (13%)
  matrix products  45.4 us (13%)
  starting transfers between devices  27.5 us (8%)
  other arithmetic  19.7 us (6%)
  between operations  14.3 us (4%)
    all_to_all x1, waiting for transfers between devices, shards(): lax.all_to_all(send_inputs, 'expert', split_axis=0, concat_axis=0, tiled=...  52.3 us
    all_to_all x1, waiting for transfers between devices, shards(): lax.all_to_all(input_rows.reshape(experts_here, CAP, model_width), 'exper...  51.2 us
    all_to_all x1, waiting for transfers between devices, shards(): lax.all_to_all(send_cot, 'expert', split_axis=0, concat_axis=0, tiled=True)  51.2 us
    reduce_scatter x1, waiting for transfers between devices, shards(): lax.psum_scatter(jnp.concatenate([gate_up_term, down_term[:, None, :]], a...  40.6 us
    dot_general x1, matrix products, shards(): jnp.einsum('mkh,hkd->md', deltas, gate_up_rows, preferred_element_type=jn...  9.99 us
    dot_general x1, matrix products, shards(): jnp.einsum('md,hkd->mkh', token_rows, gate_up_rows, preferred_element_typ...  7.6 us
    gather x2, local copies, waits for them, and re-layouts, shards(): flat_back[target_safe]  7.42 us
    all_to_all x1, starting transfers between devices, shards(): lax.all_to_all(send_scale, 'expert', split_axis=0, concat_axis=0, tiled=T...  7.25 us
  transfers between devices with their start and end apart: 6, of which 4 were waited for; matrix products, arithmetic and copies ran while one was open for 14% of the time, Pallas kernels for 0%

commit v1 on v0

v1 whole, which is shorter than its diff:
```python
import functools

import jax
import jax.numpy as jnp
from jax import lax
from jax.experimental import pallas as pl
from jax.experimental.pallas import tpu as pltpu
from jax.sharding import PartitionSpec as P

CAP = 36
MESH = pl.DeviceIdType.MESH
F32 = jnp.float32
BF16 = jnp.bfloat16


def dispatch_kernel(
    n_dp, n_ex, send_ref, out_ref, self_sem, s_ex, r_ex, s_mate, r_mate, s_y, r_y, s_fwd, r_fwd
):
    d, e = lax.axis_index("dp"), lax.axis_index("expert")
    n_y = n_dp // 2
    y, core = d // 2, lax.rem(d, 2)
    mate = d + 1 - 2 * core

    def y_peer(j):
        return lax.rem(y + j, n_y) * 2 + core

    barrier = pltpu.get_barrier_semaphore()
    for k in range(1, n_ex):
        pl.semaphore_signal(barrier, inc=1, device_id=(d, lax.rem(e + k, n_ex)), device_id_type=MESH)
    for j in range(1, n_y):
        pl.semaphore_signal(barrier, inc=1, device_id=(y_peer(j), e), device_id_type=MESH)
    pl.semaphore_signal(barrier, inc=1, device_id=(mate, e), device_id_type=MESH)
    pl.semaphore_wait(barrier, n_ex - 1 + n_y - 1 + 1)

    def source(k):
        return lax.rem(e + n_ex - k, n_ex)

    def to_expert(k):
        dest = lax.rem(e + k, n_ex)
        return pltpu.make_async_remote_copy(
            src_ref=send_ref.at[dest], dst_ref=out_ref.at[d, e], send_sem=s_ex.at[k], recv_sem=r_ex.at[k],
            device_id=(d, dest), device_id_type=MESH)

    def from_expert(k):
        return pltpu.make_async_remote_copy(
            src_ref=send_ref.at[source(k)], dst_ref=out_ref.at[d, source(k)], send_sem=s_ex.at[k],
            recv_sem=r_ex.at[k], device_id=(d, source(k)), device_id_type=MESH)

    def move(group, k, to, send_sem, recv_sem):
        slab = out_ref.at[group, source(k)]
        return pltpu.make_async_remote_copy(
            src_ref=slab, dst_ref=slab, send_sem=send_sem, recv_sem=recv_sem, device_id=(to, e),
            device_id_type=MESH)

    near = sorted(range(1, n_ex), key=lambda k: (min(k, n_ex - k), k))
    far = near[::-1]
    order = []
    for a, b in zip(far, near):
        for k in (a, b):
            if k not in order:
                order.append(k)
    own = pltpu.make_async_copy(send_ref.at[e], out_ref.at[d, e], self_sem)
    own.start()
    for k in order:
        to_expert(k).start()

    arrivals = [0] + near

    def relay(k):
        for j in range(1, n_y):
            group = lax.rem(y + n_y - j, n_y) * 2 + core
            move(group, k, mate, s_y.at[j, k], r_y.at[j, k]).wait_recv()
            move(group, k, mate, s_fwd.at[j, k], r_fwd.at[j, k]).start()

    for i, k in enumerate(arrivals):
        if k == 0:
            own.wait()
        else:
            from_expert(k).wait_recv()
        for j in range(1, n_y):
            move(d, k, y_peer(j), s_y.at[j, k], r_y.at[j, k]).start()
        move(d, k, mate, s_mate.at[k], r_mate.at[k]).start()
        if i >= 2:
            relay(arrivals[i - 2])
    for k in arrivals[-2:]:
        relay(k)
    for k in arrivals:
        move(mate, k, mate, s_mate.at[k], r_mate.at[k]).wait_recv()
        for j in range(1, n_y):
            group = lax.rem(y + n_y - j, n_y) * 2 + 1 - core
            move(group, k, mate, s_fwd.at[j, k], r_fwd.at[j, k]).wait_recv()
    for k in arrivals:
        if k:
            to_expert(k).wait_send()
        move(d, k, mate, s_mate.at[k], r_mate.at[k]).wait_send()
        for j in range(1, n_y):
            move(d, k, y_peer(j), s_y.at[j, k], r_y.at[j, k]).wait_send()
            group = lax.rem(y + n_y - j, n_y) * 2 + core
            move(group, k, mate, s_fwd.at[j, k], r_fwd.at[j, k]).wait_send()


def dispatch(send, n_dp, n_ex):
    _, rows, width = send.shape
    n_y = n_dp // 2
    dma = pltpu.SemaphoreType.DMA
    return pl.pallas_call(
        functools.partial(dispatch_kernel, n_dp, n_ex),
        out_shape=jax.ShapeDtypeStruct((n_dp, n_ex, rows, width), send.dtype),
        in_specs=[pl.BlockSpec(memory_space=pl.ANY)],
        out_specs=pl.BlockSpec(memory_space=pl.ANY),
        scratch_shapes=[
            dma, dma((n_ex,)), dma((n_ex,)), dma((n_ex,)), dma((n_ex,)),
            dma((n_y, n_ex)), dma((n_y, n_ex)), dma((n_y, n_ex)), dma((n_y, n_ex)),
        ],
        compiler_params=pltpu.CompilerParams(collective_id=0, has_side_effects=True),
    )(send)


def activations(pre_tok, pre_cot, hid):
    gate_pre, up_pre = pre_tok[..., :hid], pre_tok[..., hid : 2 * hid]
    grad_hidden = pre_cot[..., 2 * hid :]
    logistic = jax.nn.sigmoid(gate_pre)
    hidden = (gate_pre * logistic * up_pre).astype(BF16)
    gate_delta = (grad_hidden * up_pre * logistic * (1.0 + gate_pre * (1.0 - logistic))).astype(BF16)
    up_delta = (grad_hidden * gate_pre * logistic).astype(BF16)
    return hidden, grad_hidden, gate_delta, up_delta


def shards(tokens, cotangent, expert_ids, route_weights, expert_weights):
    n_ex, n_dp = lax.axis_size("expert"), lax.axis_size("dp")
    tok_rows, width = tokens.shape
    hid = expert_weights.shape[1]
    part = hid // n_dp
    slab = 2 * CAP
    half = width // 2

    columns = jnp.arange(n_ex, dtype=jnp.int32)
    chosen = expert_ids[:, :, None] == columns
    member = jnp.any(chosen, axis=1)
    scale16 = route_weights.astype(BF16).astype(F32)
    scale_te = jnp.sum(jnp.where(chosen, scale16[:, :, None], 0.0), axis=1)
    lower = (jnp.arange(tok_rows)[:, None] > jnp.arange(tok_rows)[None, :]).astype(BF16)
    slot_te = jnp.dot(lower, member.astype(BF16), preferred_element_type=F32).astype(jnp.int32)
    slot = jnp.where(member, slot_te, -1).T
    lanes = jnp.arange(slab, dtype=jnp.int32)[None, :, None]
    pick_tok = (slot[:, None, :] == lanes)
    pick_cot = (slot[:, None, :] == lanes - CAP) & (lanes >= CAP)
    pick_tok = pick_tok & (lanes < CAP)
    row_scale = jnp.sum(jnp.where(pick_cot, scale_te.T[:, None, :], 0.0), axis=2).reshape(-1, 1)
    pick_tok16 = pick_tok.astype(BF16).reshape(-1, tok_rows)
    pick_cot16 = pick_cot.astype(BF16).reshape(-1, tok_rows)
    send = (
        jnp.dot(pick_tok16, tokens, preferred_element_type=F32)
        + row_scale * jnp.dot(pick_cot16, cotangent, preferred_element_type=F32)
    ).astype(BF16)

    rows = dispatch(send.reshape(n_ex, slab, width), n_dp, n_ex)
    d = lax.axis_index("dp")
    weights = jnp.transpose(expert_weights[0], (1, 0, 2))
    flat_weights = weights.reshape(3 * hid, width)

    mine = lax.dynamic_index_in_dim(rows, d, 0, keepdims=False).reshape(n_ex * slab, width)
    pre = lax.dot_general(mine, flat_weights, (((1,), (1,)), ((), ())), preferred_element_type=F32)
    pre = pre.reshape(n_ex, slab, 3 * hid)
    hidden, grad_hidden, gate_delta, up_delta = activations(pre[:, :CAP], pre[:, CAP:], hid)
    route_rows = jnp.sum(hidden.astype(F32) * grad_hidden, axis=2)
    deltas = jnp.concatenate([gate_delta, up_delta], axis=2)
    nothing = jnp.zeros_like(deltas)
    left = jnp.concatenate([deltas, nothing], axis=1).reshape(n_ex * slab, 2 * hid)
    right = jnp.concatenate([nothing, deltas], axis=1).reshape(n_ex * slab, 2 * hid)
    input_rows = (
        jnp.dot(left, flat_weights[: 2 * hid, :half], preferred_element_type=F32)
        + jnp.dot(right, flat_weights[: 2 * hid, half:], preferred_element_type=F32)
    ).astype(BF16)
    back = lax.all_to_all(
        input_rows.reshape(n_ex, slab, half), "expert", split_axis=0, concat_axis=0, tiled=True
    )
    back_route = lax.all_to_all(route_rows, "expert", split_axis=0, concat_axis=0, tiled=True)

    own_weights = lax.dynamic_slice_in_dim(weights, d * part, part, axis=1).reshape(3 * part, width)
    every = rows.reshape(n_dp * n_ex * slab, width)
    pre_all = lax.dot_general(every, own_weights, (((1,), (1,)), ((), ())), preferred_element_type=F32)
    pre_all = pre_all.reshape(n_dp * n_ex, slab, 3 * part)
    hidden_a, _, gate_a, up_a = activations(pre_all[:, :CAP], pre_all[:, CAP:], part)
    top = jnp.concatenate([gate_a, up_a, jnp.zeros_like(hidden_a)], axis=2)
    bottom = jnp.concatenate([jnp.zeros_like(gate_a), jnp.zeros_like(up_a), hidden_a], axis=2)
    factors = jnp.concatenate([top, bottom], axis=1).reshape(-1, 3 * part)
    weight_grad = lax.dot_general(factors, every, (((0,), (0,)), ((), ())), preferred_element_type=F32)
    weight_grad = jnp.transpose(weight_grad.reshape(3, part, width), (1, 0, 2))

    back = back.reshape(n_ex * slab, half)
    input_grad = jnp.concatenate(
        [
            lax.dot_general(p, back, (((0,), (0,)), ((), ())), preferred_element_type=F32).astype(BF16)
            for p in (pick_tok16, pick_cot16)
        ],
        axis=1,
    )
    route_te = jnp.sum(jnp.where(pick_tok[:, :CAP], back_route[:, :, None], 0.0), axis=1).T
    route_grad = (
        jnp.sum(jnp.where(chosen, route_te[:, None, :], 0.0), axis=2) / scale16
    ).astype(BF16)
    return (input_grad, route_grad, weight_grad[None])


def solution(mesh):
    in_specs = (
        P(("dp", "expert"), None),
        P(("dp", "expert"), None),
        P(("dp", "expert"), None),
        P(("dp", "expert"), None),
        P("expert", None, None, None),
    )
    out_specs = (
        P(("dp", "expert"), None),
        P(("dp", "expert"), None),
        P("expert", "dp", None, None),
    )
    return jax.shard_map(shards, mesh=mesh, in_specs=in_specs, out_specs=out_specs, check_vma=False)
```

time: 348 us -> 295 us (0.85)
  waiting for transfers between devices: 195 us -> 8.45 us
  Pallas kernels: 0 us -> 140 us
  local copies, waits for them, and re-layouts: 45.5 us -> 11.4 us
  matrix products: 45.4 us -> 77.9 us
  starting transfers between devices: 27.5 us -> 45.8 us
  between operations: 14.3 us -> 0.85 us
  other arithmetic: 19.7 us -> 10.5 us
    all_to_all x5 -> x2, waiting for transfers between devices: 155 us -> 8.45 us  [the longest x1 8.45 us: shards(): lax.all_to_all(input_rows.reshape(n_ex, slab, half), 'expert', split_axis...]
    pallas_call x0 -> x1, Pallas kernels: none -> 140 us  [dispatch(): pl.pallas_call(functools.partial(dispatch_kernel, n_dp, n_ex), out_shape=...]
    reduce_scatter x1 -> x0, waiting for transfers between devices: 40.6 us -> none  [shards(): lax.psum_scatter(jnp.concatenate([gate_up_term, down_term[:, None, :]], a...]
    dot_general x8 -> x10, matrix products: 45.4 us -> 77.9 us  [the longest x1 19.4 us: shards(): lax.dot_general(every, own_weights, (((1,), (1,)), ((), ())), preferred_e...]
    reshape x8 -> x0, local copies, waits for them, and re-layouts: 18.9 us -> none  [the longest x1 4.12 us: shards(): token_rows = recv_inputs.reshape(-1, model_width)]
    all_to_all x5 -> x2, starting transfers between devices: 27.3 us -> 45.8 us  [the longest x1 39.8 us: shards(): lax.all_to_all(route_rows, 'expert', split_axis=0, concat_axis=0, tiled=T...]
    gather x3 -> x0, local copies, waits for them, and re-layouts: 9.89 us -> none  [the longest x2 7.42 us: shards(): flat_back[target_safe]]
    broadcast_in_dim x1 -> x0, other arithmetic: 6.95 us -> none  [shards(): return (input_grad, route_grad, summed[None])]
  transfers between devices with their start and end apart: 6 -> 2, of which waited for: 4 -> 1; matrix products, arithmetic and copies ran while one was open for 14% -> 22% of each run, Pallas kernels for 0% -> 0%
where the time goes in v1:
time: 295 us
  Pallas kernels  140 us (47%)
  matrix products  77.9 us (26%)
  starting transfers between devices  45.8 us (16%)
  local copies, waits for them, and re-layouts  11.4 us (4%)
  other arithmetic  10.5 us (4%)
  waiting for transfers between devices  8.45 us (3%)
    pallas_call x1, Pallas kernels, dispatch(): pl.pallas_call(functools.partial(dispatch_kernel, n_dp, n_ex), out_shape=...  140 us
    all_to_all x1, starting transfers between devices, shards(): lax.all_to_all(route_rows, 'expert', split_axis=0, concat_axis=0, tiled=T...  39.8 us
    dot_general x1, matrix products, shards(): lax.dot_general(every, own_weights, (((1,), (1,)), ((), ())), preferred_e...  19.4 us
    dot_general x1, matrix products, shards(): lax.dot_general(mine, flat_weights, (((1,), (1,)), ((), ())), preferred_e...  16.9 us
    dot_general x1, matrix products, shards(): lax.dot_general(factors, every, (((0,), (0,)), ((), ())), preferred_eleme...  16.8 us
    all_to_all x1, waiting for transfers between devices, shards(): lax.all_to_all(input_rows.reshape(n_ex, slab, half), 'expert', split_axis...  8.45 us
    dot_general x1, matrix products, shards(): jnp.dot(left, flat_weights[:2 * hid, :half], preferred_element_type=F32)  7.84 us
    dot_general x1, matrix products, shards(): jnp.dot(right, flat_weights[:2 * hid, half:], preferred_element_type=F32)  6.32 us
  transfers between devices with their start and end apart: 2, of which 1 were waited for; matrix products, arithmetic and copies ran while one was open for 22% of the time, Pallas kernels for 0%

profile of v1, /device:TPU:0, one launch (start us, length us, event | category | flops | bytes accessed | tf_op | source)
XLA Modules:
  0.0 294.9 jit_solution(18367354363777284572)
XLA Ops:
  0.9 0.8 fusion.20
  2.0 0.7 convert_convert_fusion
  2.8 0.7 select_reduce_fusion.3
  4.3 1.4 fusion.24
  5.7 3.8 %add_convert_fusion = bf16[576,4096]{1,0:T(8,128)(2,1)} fusion(f32[576,4096]{1,0:T(8,128)S(1)} %fusion.24, pred[576,192]{1,0:T(32,128)(4,1)S(1)} %get-tuple-element.11, bf16[192,4096]{1,0:T(8,128)(2,1)S(1)} %copy-done.2, f32[576]{0:T(1024)S(1)} %mul.64), kind=kOutput, calls=%fused_computation | convolution fusion | flops 913047552 | bytes 15841536 | tf_op jit(solution)/shard_map/dot_general | solution.py:154
  9.5 140.1 %shard_map.76 = bf16[4,8,72,4096]{3,2,1,0:T(8,128)(2,1)} custom-call(bf16[8,72,4096]{2,1,0:T(8,128)(2,1)} %bitcast.68), custom_call_target="tpu_custom_call" | custom-call | tf_op jit(solution)/shard_map/pallas_call | solution.py:106
  149.5 16.9 %fusion.5 = f32[8,72,2112]{2,1,0:T(8,128)S(1)} fusion(bf16[2112,4096,1]{1,0,2:T(8,128)(2,1)} %bitcast.77, bf16[4,8,72,4096]{3,2,1,0:T(8,128)(2,1)} %shard_map.76, s32[]{:T(128)S(6)} %select_n.31), kind=kOutput, calls=%fused_computation.8 | convolution fusion | flops 9965666304 | bytes 26886148 | tf_op jit(solution)/shard_map/dot_general | solution.py:163
  166.4 1.4 multiply_reduce_fusion
  167.9 39.8 %all-to-all-start.1 = ((f32[8,1,36]{2,1,0:T(1,128)}), f32[8,1,36]{2,1,0:T(1,128)S(1)}, u32[]{:S(2)}, u32[]{:S(2)}) async-start(f32[8,1,36]{2,1,0:T(1,128)} %bitcast.16), calls=%async_computation.1 | async-start | bytes 8192 | tf_op jit(solution)/shard_map/all_to_all | solution.py:178
  207.9 1.5 fusion.23
  209.5 6.3 %fusion.1 = f32[576,2048]{1,0:T(8,128)S(1)} fusion(bf16[576,1408]{1,0:T(8,128)(2,1)} %bitcast.76, bf16[2112,4096]{1,0:T(8,128)(2,1)} %bitcast.78), kind=kOutput, calls=%fused_computation.4 | convolution fusion | flops 3321888768 | bytes 12107776 | tf_op jit(solution)/shard_map/dot_general | solution.py:173
  215.8 7.8 %add_convert_fusion.1 = bf16[576,2048]{1,0:T(8,128)(2,1)} fusion(f32[576,2048]{1,0:T(8,128)S(1)} %fusion.1, bf16[576,1408]{1,0:T(8,128)(2,1)S(1)} %bitcast.75, bf16[2112,4096]{1,0:T(8,128)(2,1)} %bitcast.79), kind=kOutput, calls=%fused_computation.10 | convolution fusion | flops 3324248064 | bytes 14467072 | tf_op jit(solution)/shard_map/dot_general | solution.py:172
  223.6 4.8 %constant_dynamic-slice_fusion = bf16[1,176,3,4096]{3,1,2,0:T(8,128)(2,1)} fusion(bf16[1,704,3,4096]{3,1,2,0:T(8,128)(2,1)} %param.9, s32[]{:T(128)S(6)} %select_n.34), kind=kLoop, calls=%fused_computation.49 | loop fusion | bytes 8650756 | tf_op jit(solution)/shard_map/dynamic-slice.1
  228.4 6.0 %all-to-all-start = ((bf16[8,72,2048]{2,1,0:T(8,128)(2,1)}), bf16[8,72,2048]{2,1,0:T(8,128)(2,1)}, u32[]{:S(2)}, u32[]{:S(2)}) async-start(bf16[8,72,2048]{2,1,0:T(8,128)(2,1)} %bitcast.74), calls=%async_computation | async-start | bytes 4718592 | tf_op jit(solution)/shard_map/all_to_all | solution.py:175
  234.4 19.4 %fusion.25 = f32[32,72,528]{2,1,0:T(8,128)S(1)} fusion(bf16[32,72,4096]{2,1,0:T(8,128)(2,1)} %bitcast.69, bf16[528,4096,1]{1,0,2:T(8,128)(2,1)} %bitcast.72), kind=kOutput, calls=%fused_computation.56 | convolution fusion | flops 9965666304 | bytes 28065792 | tf_op jit(solution)/shard_map/dot_general | solution.py:182
  253.9 1.1 multiply_convert_fusion.2
  255.0 2.7 fusion.10
  257.7 4.5 %copy.15 = bf16[528,2304]{1,0:T(8,128)(2,1)} copy(bf16[528,2304]{0,1:T(8,128)(2,1)} %bitcast.71) | data formatting | bytes 4866048 | tf_op jit(solution)/shard_map/dot_general | solution.py:188
  262.3 16.8 %convolution_bitcast_fusion = f32[1,176,3,4096]{3,1,2,0:T(8,128)} fusion(bf16[3,176,2304]{2,1,0:T(8,128)(2,1)} %bitcast.73, bf16[2304,4096,1]{1,0,2:T(8,128)(2,1)} %bitcast.70), kind=kOutput, calls=%fused_computation.1 | convolution fusion | flops 9965666304 | bytes 29958144 | tf_op jit(solution)/shard_map/dot_general | solution.py:188
  279.4 0.6 divide_convert_fusion
  280.0 8.5 %all-to-all-done = bf16[8,72,2048]{2,1,0:T(8,128)(2,1)} async-done(((bf16[8,72,2048]{2,1,0:T(8,128)(2,1)}), bf16[8,72,2048]{2,1,0:T(8,128)(2,1)}, u32[]{:S(2)}, u32[]{:S(2)}) %all-to-all-start) | async-done | bytes 2359328 | tf_op jit(solution)/shard_map/all_to_all | solution.py:175
  288.4 2.7 fusion.12
  291.1 2.6 fusion.11
  293.6 1.3 pad_maximum_fusion
  (32 shorter events, 1.9 us)
Async XLA Ops:
  0.6 3.6 %copy-start = (bf16[192,4096]{1,0:T(8,128)(2,1)S(1)}, bf16[192,4096]{1,0:T(8,128)(2,1)}, u32[]{:S(2)}) copy-start(bf16[192,4096]{1,0:T(8,128)(2,1)} %param.5) | copy-start | bytes 4718596
  4.3 1.4 copy-start.2
  167.9 60.5 %all-to-all-start.1 = ((f32[8,1,36]{2,1,0:T(1,128)}), f32[8,1,36]{2,1,0:T(1,128)S(1)}, u32[]{:S(2)}, u32[]{:S(2)}) async-start(f32[8,1,36]{2,1,0:T(1,128)} %bitcast.16), calls=%async_computation.1 | async-start | bytes 8192 | tf_op jit(solution)/shard_map/all_to_all | solution.py:178
  228.4 60.0 %all-to-all-start = ((bf16[8,72,2048]{2,1,0:T(8,128)(2,1)}), bf16[8,72,2048]{2,1,0:T(8,128)(2,1)}, u32[]{:S(2)}, u32[]{:S(2)}) async-start(bf16[8,72,2048]{2,1,0:T(8,128)(2,1)} %bitcast.74), calls=%async_computation | async-start | bytes 4718592 | tf_op jit(solution)/shard_map/all_to_all | solution.py:175
  262.3 17.0 %copy-start.3 = (s32[192,6]{0,1:T(8,128)S(1)}, s32[192,6]{0,1:T(8,128)}, u32[]{:S(2)}) copy-start(s32[192,6]{0,1:T(8,128)} %param.7) | copy-start | bytes 13828
  262.3 17.0 %copy-start.4 = (f32[192,6]{0,1:T(8,128)S(1)}, f32[192,6]{0,1:T(8,128)}, u32[]{:S(2)}) copy-start(f32[192,6]{0,1:T(8,128)} %param.8) | copy-start | bytes 13828
  288.4 6.5 %copy-start.1 = (bf16[192,4096]{1,0:T(8,128)(2,1)S(1)}, bf16[192,4096]{1,0:T(8,128)(2,1)}, u32[]{:S(2)}) copy-start(bf16[192,4096]{1,0:T(8,128)(2,1)} %param.5) | copy-start | bytes 4718596

commit v2 on v1

--- a/solution.py
+++ b/solution.py
@@ -17,9 +17,10 @@
     n_dp, n_ex, send_ref, out_ref, self_sem, s_ex, r_ex, s_mate, r_mate, s_y, r_y, s_fwd, r_fwd
 ):
     d, e = lax.axis_index("dp"), lax.axis_index("expert")
-    n_y = n_dp // 2
+    n_y, half = n_dp // 2, n_ex // 2
     y, core = d // 2, lax.rem(d, 2)
     mate = d + 1 - 2 * core
+    side, place = e // half, lax.rem(e, half)
 
     def y_peer(j):
         return lax.rem(y + j, n_y) * 2 + core
@@ -32,76 +33,94 @@
     pl.semaphore_signal(barrier, inc=1, device_id=(mate, e), device_id_type=MESH)
     pl.semaphore_wait(barrier, n_ex - 1 + n_y - 1 + 1)
 
-    def source(k):
-        return lax.rem(e + n_ex - k, n_ex)
-
-    def to_expert(k):
-        dest = lax.rem(e + k, n_ex)
+    def across(far):
+        return (1 - side) * half if far else side * half
+
+    def to_expert(far, r):
+        dest = across(far) + lax.rem(place + r, half)
         return pltpu.make_async_remote_copy(
-            src_ref=send_ref.at[dest], dst_ref=out_ref.at[d, e], send_sem=s_ex.at[k], recv_sem=r_ex.at[k],
-            device_id=(d, dest), device_id_type=MESH)
-
-    def from_expert(k):
+            src_ref=send_ref.at[dest], dst_ref=out_ref.at[d, e], send_sem=s_ex.at[far, r],
+            recv_sem=r_ex.at[far, r], device_id=(d, dest), device_id_type=MESH)
+
+    def source(far, r):
+        return across(far) + lax.rem(place + half - r, half)
+
+    def from_expert(far, r):
+        src = source(far, r)
         return pltpu.make_async_remote_copy(
-            src_ref=send_ref.at[source(k)], dst_ref=out_ref.at[d, source(k)], send_sem=s_ex.at[k],
-            recv_sem=r_ex.at[k], device_id=(d, source(k)), device_id_type=MESH)
-
-    def move(group, k, to, send_sem, recv_sem):
-        slab = out_ref.at[group, source(k)]
+            src_ref=send_ref.at[src], dst_ref=out_ref.at[d, src], send_sem=s_ex.at[far, r],
+            recv_sem=r_ex.at[far, r], device_id=(d, src), device_id_type=MESH)
+
+    def move(group, far, r, to, send_sem, recv_sem):
+        slab = out_ref.at[group, source(far, r)]
         return pltpu.make_async_remote_copy(
             src_ref=slab, dst_ref=slab, send_sem=send_sem, recv_sem=recv_sem, device_id=(to, e),
             device_id_type=MESH)
 
-    near = sorted(range(1, n_ex), key=lambda k: (min(k, n_ex - k), k))
-    far = near[::-1]
-    order = []
-    for a, b in zip(far, near):
-        for k in (a, b):
-            if k not in order:
-                order.append(k)
+    def to_mate(group, far, r):
+        return move(group, far, r, mate, s_mate.at[far, r], r_mate.at[far, r])
+
+    def to_y(group, far, r, j):
+        return move(group, far, r, y_peer(j), s_y.at[j, far, r], r_y.at[j, far, r])
+
+    def pass_on(group, far, r, j):
+        return move(group, far, r, mate, s_fwd.at[j, far, r], r_fwd.at[j, far, r])
+
+    def y_source(j):
+        return lax.rem(y + n_y - j, n_y) * 2
+
+    def forward(far, r):
+        if not far and r == 0:
+            own.wait()
+        else:
+            from_expert(far, r).wait_recv()
+        for j in range(1, n_y):
+            to_y(d, far, r, j).start()
+        to_mate(d, far, r).start()
+
+    def relay(far, r):
+        for j in range(1, n_y):
+            to_y(y_source(j) + core, far, r, j).wait_recv()
+            pass_on(y_source(j) + core, far, r, j).start()
+
     own = pltpu.make_async_copy(send_ref.at[e], out_ref.at[d, e], self_sem)
     own.start()
-    for k in order:
-        to_expert(k).start()
-
-    arrivals = [0] + near
-
-    def relay(k):
-        for j in range(1, n_y):
-            group = lax.rem(y + n_y - j, n_y) * 2 + core
-            move(group, k, mate, s_y.at[j, k], r_y.at[j, k]).wait_recv()
-            move(group, k, mate, s_fwd.at[j, k], r_fwd.at[j, k]).start()
-
-    for i, k in enumerate(arrivals):
-        if k == 0:
-            own.wait()
-        else:
-            from_expert(k).wait_recv()
-        for j in range(1, n_y):
-            move(d, k, y_peer(j), s_y.at[j, k], r_y.at[j, k]).start()
-        move(d, k, mate, s_mate.at[k], r_mate.at[k]).start()
-        if i >= 2:
-            relay(arrivals[i - 2])
-    for k in arrivals[-2:]:
-        relay(k)
-    for k in arrivals:
-        move(mate, k, mate, s_mate.at[k], r_mate.at[k]).wait_recv()
-        for j in range(1, n_y):
-            group = lax.rem(y + n_y - j, n_y) * 2 + 1 - core
-            move(group, k, mate, s_fwd.at[j, k], r_fwd.at[j, k]).wait_recv()
-    for k in arrivals:
-        if k:
-            to_expert(k).wait_send()
-        move(d, k, mate, s_mate.at[k], r_mate.at[k]).wait_send()
-        for j in range(1, n_y):
-            move(d, k, y_peer(j), s_y.at[j, k], r_y.at[j, k]).wait_send()
-            group = lax.rem(y + n_y - j, n_y) * 2 + core
-            move(group, k, mate, s_fwd.at[j, k], r_fwd.at[j, k]).wait_send()
+    pending = []
+    for r in range(half):
+        if r:
+            to_expert(1, r - 1).wait_send()
+        to_expert(1, r).start()
+        if r + 1 < half:
+            to_expert(0, r + 1).start()
+        if r:
+            forward(1, r - 1)
+            pending.append((1, r - 1))
+        forward(0, r)
+        pending.append((0, r))
+        while len(pending) > 4:
+            relay(*pending.pop(0))
+    forward(1, half - 1)
+    pending.append((1, half - 1))
+    for flow in pending:
+        relay(*flow)
+    flows = [(far, r) for r in range(half) for far in (0, 1)]
+    for flow in flows:
+        to_mate(mate, *flow).wait_recv()
+        for j in range(1, n_y):
+            pass_on(y_source(j) + 1 - core, *flow, j).wait_recv()
+    to_expert(1, half - 1).wait_send()
+    for far, r in flows:
+        if not far and r:
+            to_expert(far, r).wait_send()
+        to_mate(d, far, r).wait_send()
+        for j in range(1, n_y):
+            to_y(d, far, r, j).wait_send()
+            pass_on(y_source(j) + core, far, r, j).wait_send()
 
 
 def dispatch(send, n_dp, n_ex):
     _, rows, width = send.shape
-    n_y = n_dp // 2
+    n_y, half = n_dp // 2, n_ex // 2
     dma = pltpu.SemaphoreType.DMA
     return pl.pallas_call(
         functools.partial(dispatch_kernel, n_dp, n_ex),
@@ -109,8 +128,8 @@
         in_specs=[pl.BlockSpec(memory_space=pl.ANY)],
         out_specs=pl.BlockSpec(memory_space=pl.ANY),
         scratch_shapes=[
-            dma, dma((n_ex,)), dma((n_ex,)), dma((n_ex,)), dma((n_ex,)),
-            dma((n_y, n_ex)), dma((n_y, n_ex)), dma((n_y, n_ex)), dma((n_y, n_ex)),
+            dma, dma((2, half)), dma((2, half)), dma((2, half)), dma((2, half)),
+            dma((n_y, 2, half)), dma((n_y, 2, half)), dma((n_y, 2, half)), dma((n_y, 2, half)),
         ],
         compiler_params=pltpu.CompilerParams(collective_id=0, has_side_effects=True),
     )(send)
@@ -175,7 +194,8 @@
     back = lax.all_to_all(
         input_rows.reshape(n_ex, slab, half), "expert", split_axis=0, concat_axis=0, tiled=True
     )
-    back_route = lax.all_to_all(route_rows, "expert", split_axis=0, concat_axis=0, tiled=True)
+    all_route = lax.all_gather(route_rows, "expert", axis=0, tiled=False)
+    back_route = lax.dynamic_index_in_dim(all_route, lax.axis_index("expert"), 1, keepdims=False)
 
     own_weights = lax.dynamic_slice_in_dim(weights, d * part, part, axis=1).reshape(3 * part, width)
     every = rows.reshape(n_dp * n_ex * slab, width)

time: 295 us -> 285 us (0.966)
  blocking collectives: 0 us -> 41.8 us
  starting transfers between devices: 45.8 us -> 4.59 us
  waiting for transfers between devices: 8.45 us -> 0.01 us
  local copies, waits for them, and re-layouts: 11.4 us -> 8.19 us
    all_gather x0 -> x1, blocking collectives: none -> 41.8 us  [shards(): all_route = lax.all_gather(route_rows, 'expert', axis=0, tiled=False)]
    all_to_all x1 -> x0, starting transfers between devices: 39.8 us -> none  [shards(): lax.all_to_all(route_rows, 'expert', split_axis=0, concat_axis=0, tiled=T...]
    all_to_all x1, waiting for transfers between devices: 8.45 us -> 0.01 us  [shards(): lax.all_to_all(input_rows.reshape(n_ex, slab, half), 'expert', split_axis...]
  transfers between devices with their start and end apart: 2 -> 1, of which waited for: 1 -> 0; matrix products, arithmetic and copies ran while one was open for 22% -> 18% of each run, Pallas kernels for 0% -> 0%
where the time goes in v2:
time: 285 us; the launch traced here: 284 us
  Pallas kernels  139 us (49%)
  matrix products  77.1 us (27%)
  blocking collectives  41.8 us (15%)
  other arithmetic  12.4 us (4%)
  local copies, waits for them, and re-layouts  8.19 us (3%)
  starting transfers between devices  4.59 us (2%)
    pallas_call x1, Pallas kernels, dispatch(): pl.pallas_call(functools.partial(dispatch_kernel, n_dp, n_ex), out_shape=...  139 us
    all_gather x1, blocking collectives, shards(): all_route = lax.all_gather(route_rows, 'expert', axis=0, tiled=False)  41.8 us
    dot_general x1, matrix products, shards(): lax.dot_general(every, own_weights, (((1,), (1,)), ((), ())), preferred_e...  19 us
    dot_general x1, matrix products, shards(): lax.dot_general(mine, flat_weights, (((1,), (1,)), ((), ())), preferred_e...  17.1 us
    dot_general x1, matrix products, shards(): lax.dot_general(factors, every, (((0,), (0,)), ((), ())), preferred_eleme...  16.8 us
    dot_general x1, matrix products, shards(): jnp.dot(left, flat_weights[:2 * hid, :half], preferred_element_type=F32)  7.84 us
    dot_general x1, matrix products, shards(): jnp.dot(right, flat_weights[:2 * hid, half:], preferred_element_type=F32)  5.84 us
  transfers between devices with their start and end apart: 1, of which 0 were waited for; matrix products, arithmetic and copies ran while one was open for 18% of the time, Pallas kernels for 0%

profile of v2, /device:TPU:0, one launch (start us, length us, event | category | flops | bytes accessed | tf_op | source)
XLA Modules:
  0.0 284.1 jit_solution(11080931299547697059)
XLA Ops:
  0.9 0.8 fusion.20
  2.0 0.7 convert_convert_fusion
  2.8 0.7 select_reduce_fusion.3
  3.9 0.4 fusion.16
  4.3 1.4 fusion.24
  5.7 3.8 %add_convert_fusion = bf16[576,4096]{1,0:T(8,128)(2,1)} fusion(f32[576,4096]{1,0:T(8,128)S(1)} %fusion.24, pred[576,192]{1,0:T(32,128)(4,1)S(1)} %get-tuple-element.11, bf16[192,4096]{1,0:T(8,128)(2,1)S(1)} %copy-done.2, f32[576]{0:T(1024)S(1)} %mul.64), kind=kOutput, calls=%fused_computation | convolution fusion | flops 913047552 | bytes 15841536 | tf_op jit(solution)/shard_map/dot_general | solution.py:173
  9.5 139.2 %shard_map.76 = bf16[4,8,72,4096]{3,2,1,0:T(8,128)(2,1)} custom-call(bf16[8,72,4096]{2,1,0:T(8,128)(2,1)} %bitcast.68), custom_call_target="tpu_custom_call" | custom-call | tf_op jit(solution)/shard_map/pallas_call | solution.py:125
  148.7 17.1 %fusion.5 = f32[8,72,2112]{2,1,0:T(8,128)S(1)} fusion(bf16[2112,4096,1]{1,0,2:T(8,128)(2,1)} %bitcast.77, bf16[4,8,72,4096]{3,2,1,0:T(8,128)(2,1)} %shard_map.76, s32[]{:T(128)S(6)} %select_n.35), kind=kOutput, calls=%fused_computation.8 | convolution fusion | flops 9965666304 | bytes 26886148 | tf_op jit(solution)/shard_map/dot_general | solution.py:182
  165.7 0.8 multiply_reduce_fusion
  166.8 0.4 fusion.23
  167.2 5.8 %fusion.1 = f32[576,2048]{1,0:T(8,128)S(1)} fusion(bf16[576,1408]{1,0:T(8,128)(2,1)S(1)} %bitcast.76, bf16[2112,4096]{1,0:T(8,128)(2,1)} %bitcast.78), kind=kOutput, calls=%fused_computation.4 | convolution fusion | flops 3321888768 | bytes 12107776 | tf_op jit(solution)/shard_map/dot_general | solution.py:192
  173.1 7.8 %add_convert_fusion.1 = bf16[576,2048]{1,0:T(8,128)(2,1)} fusion(f32[576,2048]{1,0:T(8,128)S(1)} %fusion.1, bf16[576,1408]{1,0:T(8,128)(2,1)S(1)} %bitcast.75, bf16[2112,4096]{1,0:T(8,128)(2,1)} %bitcast.79), kind=kOutput, calls=%fused_computation.10 | convolution fusion | flops 3324248064 | bytes 14467072 | tf_op jit(solution)/shard_map/dot_general | solution.py:191
  180.9 4.6 %all-to-all-start = ((bf16[8,72,2048]{2,1,0:T(8,128)(2,1)}), bf16[8,72,2048]{2,1,0:T(8,128)(2,1)}, u32[]{:S(2)}, u32[]{:S(2)}) async-start(bf16[8,72,2048]{2,1,0:T(8,128)(2,1)} %bitcast.74), calls=%async_computation | async-start | bytes 4718592 | tf_op jit(solution)/shard_map/all_to_all | solution.py:194
  185.5 2.7 constant_dynamic-slice_fusion
  188.3 19.0 %fusion.25 = f32[32,72,528]{2,1,0:T(8,128)} fusion(bf16[32,72,4096]{2,1,0:T(8,128)(2,1)} %bitcast.69, bf16[528,4096,1]{1,0,2:T(8,128)(2,1)S(1)} %bitcast.72), kind=kOutput, calls=%fused_computation.57 | convolution fusion | flops 9965666304 | bytes 28065792 | tf_op jit(solution)/shard_map/dot_general | solution.py:202
  207.4 3.5 %multiply_convert_fusion.2 = (bf16[32,36,176]{2,1,0:T(8,128)(2,1)S(1)}, bf16[32,36,176]{2,1,0:T(8,128)(2,1)S(1)}, bf16[32,36,176]{2,1,0:T(8,128)(2,1)S(1)}) fusion(f32[32,72,528]{2,1,0:T(8,128)} %fusion.25), kind=kLoop, calls=%fused_computation.20 | loop fusion | flops 3244032 | bytes 3649536 | tf_op jit(solution)/shard_map/convert_element_type | solution.py:143
  210.9 2.7 fusion.10
  213.5 4.5 %copy.18 = bf16[528,2304]{1,0:T(8,128)(2,1)} copy(bf16[528,2304]{0,1:T(8,128)(2,1)} %bitcast.71) | data formatting | bytes 4866048 | tf_op jit(solution)/shard_map/dot_general | solution.py:208
  218.1 41.8 %all-gather = f32[64,36]{1,0:T(8,128)S(1)} all-gather(f32[8,36]{1,0:T(8,128)S(1)} %get-tuple-element.6), channel_id=2, replica_groups=mesh['dp'=4,'expert'=8] {'expert'}, dimensions={0}, use_global_device_ids=true | all-gather | bytes 10368 | tf_op jit(solution)/shard_map/all_gather | solution.py:197
  260.2 0.6 divide_convert_fusion
  260.8 16.8 %convolution_bitcast_fusion = f32[1,176,3,4096]{3,1,2,0:T(8,128)} fusion(bf16[3,176,2304]{2,1,0:T(8,128)(2,1)} %bitcast.73, bf16[2304,4096,1]{1,0,2:T(8,128)(2,1)} %bitcast.70), kind=kOutput, calls=%fused_computation.1 | convolution fusion | flops 9965666304 | bytes 29958144 | tf_op jit(solution)/shard_map/dot_general | solution.py:208
  277.6 2.7 fusion.12
  280.3 2.6 fusion.11
  282.9 1.3 pad_maximum_fusion
  (32 shorter events, 1.6 us)
Async XLA Ops:
  0.6 3.6 %copy-start = (bf16[192,4096]{1,0:T(8,128)(2,1)S(1)}, bf16[192,4096]{1,0:T(8,128)(2,1)}, u32[]{:S(2)}) copy-start(bf16[192,4096]{1,0:T(8,128)(2,1)} %param.5) | copy-start | bytes 4718596
  4.3 1.4 copy-start.2
  180.9 96.7 %all-to-all-start = ((bf16[8,72,2048]{2,1,0:T(8,128)(2,1)}), bf16[8,72,2048]{2,1,0:T(8,128)(2,1)}, u32[]{:S(2)}, u32[]{:S(2)}) async-start(bf16[8,72,2048]{2,1,0:T(8,128)(2,1)} %bitcast.74), calls=%async_computation | async-start | bytes 4718592 | tf_op jit(solution)/shard_map/all_to_all | solution.py:194
  213.5 46.6 %copy-start.3 = (s32[192,6]{0,1:T(8,128)S(1)}, s32[192,6]{0,1:T(8,128)}, u32[]{:S(2)}) copy-start(s32[192,6]{0,1:T(8,128)} %param.7) | copy-start | bytes 13828
  213.5 46.7 %copy-start.4 = (f32[192,6]{0,1:T(8,128)S(1)}, f32[192,6]{0,1:T(8,128)}, u32[]{:S(2)}) copy-start(f32[192,6]{0,1:T(8,128)} %param.8) | copy-start | bytes 13828
  277.6 6.5 %copy-start.1 = (bf16[192,4096]{1,0:T(8,128)(2,1)S(1)}, bf16[192,4096]{1,0:T(8,128)(2,1)}, u32[]{:S(2)}) copy-start(bf16[192,4096]{1,0:T(8,128)(2,1)} %param.5) | copy-start | bytes 4718596

commit v3 on v2

--- a/solution.py
+++ b/solution.py
@@ -33,89 +33,100 @@
     pl.semaphore_signal(barrier, inc=1, device_id=(mate, e), device_id_type=MESH)
     pl.semaphore_wait(barrier, n_ex - 1 + n_y - 1 + 1)
 
+    cols = send_ref.shape[2] // 2
+
     def across(far):
         return (1 - side) * half if far else side * half
 
-    def to_expert(far, r):
+    def to_expert(far, r, h):
         dest = across(far) + lax.rem(place + r, half)
+        piece = pl.ds(h * cols, cols)
         return pltpu.make_async_remote_copy(
-            src_ref=send_ref.at[dest], dst_ref=out_ref.at[d, e], send_sem=s_ex.at[far, r],
-            recv_sem=r_ex.at[far, r], device_id=(d, dest), device_id_type=MESH)
+            src_ref=send_ref.at[dest, :, piece], dst_ref=out_ref.at[d, e, :, piece],
+            send_sem=s_ex.at[far, r, h], recv_sem=r_ex.at[far, r, h], device_id=(d, dest), device_id_type=MESH)
 
     def source(far, r):
         return across(far) + lax.rem(place + half - r, half)
 
-    def from_expert(far, r):
+    def from_expert(far, r, h):
         src = source(far, r)
+        piece = pl.ds(h * cols, cols)
         return pltpu.make_async_remote_copy(
-            src_ref=send_ref.at[src], dst_ref=out_ref.at[d, src], send_sem=s_ex.at[far, r],
-            recv_sem=r_ex.at[far, r], device_id=(d, src), device_id_type=MESH)
-
-    def move(group, far, r, to, send_sem, recv_sem):
-        slab = out_ref.at[group, source(far, r)]
+            src_ref=send_ref.at[src, :, piece], dst_ref=out_ref.at[d, src, :, piece],
+            send_sem=s_ex.at[far, r, h], recv_sem=r_ex.at[far, r, h], device_id=(d, src), device_id_type=MESH)
+
+    def move(group, far, r, h, to, send_sem, recv_sem):
+        slab = out_ref.at[group, source(far, r), :, pl.ds(h * cols, cols)]
         return pltpu.make_async_remote_copy(
             src_ref=slab, dst_ref=slab, send_sem=send_sem, recv_sem=recv_sem, device_id=(to, e),
             device_id_type=MESH)
 
-    def to_mate(group, far, r):
-        return move(group, far, r, mate, s_mate.at[far, r], r_mate.at[far, r])
-
-    def to_y(group, far, r, j):
-        return move(group, far, r, y_peer(j), s_y.at[j, far, r], r_y.at[j, far, r])
-
-    def pass_on(group, far, r, j):
-        return move(group, far, r, mate, s_fwd.at[j, far, r], r_fwd.at[j, far, r])
+    def to_mate(group, far, r, h):
+        return move(group, far, r, h, mate, s_mate.at[far, r, h], r_mate.at[far, r, h])
+
+    def to_y(group, far, r, h, j):
+        return move(group, far, r, h, y_peer(j), s_y.at[j, far, r, h], r_y.at[j, far, r, h])
+
+    def pass_on(group, far, r, h, j):
+        return move(group, far, r, h, mate, s_fwd.at[j, far, r, h], r_fwd.at[j, far, r, h])
 
     def y_source(j):
         return lax.rem(y + n_y - j, n_y) * 2
 
-    def forward(far, r):
-        if not far and r == 0:
-            own.wait()
-        else:
-            from_expert(far, r).wait_recv()
+    pending = []
+
+    def forward(far, r, h):
+        if far or r:
+            from_expert(far, r, h).wait_recv()
         for j in range(1, n_y):
-            to_y(d, far, r, j).start()
-        to_mate(d, far, r).start()
-
-    def relay(far, r):
-        for j in range(1, n_y):
-            to_y(y_source(j) + core, far, r, j).wait_recv()
-            pass_on(y_source(j) + core, far, r, j).start()
+            to_y(d, far, r, h, j).start()
+        to_mate(d, far, r, h).start()
+        pending.append((far, r, h))
+
+    def relay(lag):
+        while len(pending) > lag:
+            flow = pending.pop(0)
+            for j in range(1, n_y):
+                to_y(y_source(j) + core, *flow, j).wait_recv()
+                pass_on(y_source(j) + core, *flow, j).start()
 
     own = pltpu.make_async_copy(send_ref.at[e], out_ref.at[d, e], self_sem)
     own.start()
-    pending = []
-    for r in range(half):
-        if r:
-            to_expert(1, r - 1).wait_send()
-        to_expert(1, r).start()
-        if r + 1 < half:
-            to_expert(0, r + 1).start()
-        if r:
-            forward(1, r - 1)
-            pending.append((1, r - 1))
-        forward(0, r)
-        pending.append((0, r))
-        while len(pending) > 4:
-            relay(*pending.pop(0))
-    forward(1, half - 1)
-    pending.append((1, half - 1))
-    for flow in pending:
-        relay(*flow)
-    flows = [(far, r) for r in range(half) for far in (0, 1)]
+    far_flows = [(1, r, h) for r in range(half) for h in (0, 1)]
+    near_flows = [(0, r, h) for r in range(1, half) for h in (0, 1)]
+    for p, flow in enumerate(far_flows):
+        if p >= 2:
+            to_expert(*far_flows[p - 2]).wait_send()
+        to_expert(*flow).start()
+        if p < len(near_flows):
+            to_expert(*near_flows[p]).start()
+        if p == 0:
+            own.wait()
+            forward(0, 0, 0)
+            forward(0, 0, 1)
+        if p >= 2:
+            forward(*far_flows[p - 2])
+        if 1 <= p <= len(near_flows):
+            forward(*near_flows[p - 1])
+        relay(6)
+    forward(*far_flows[-2])
+    relay(3)
+    forward(*far_flows[-1])
+    relay(0)
+    flows = [(far, r, h) for r in range(half) for far in (0, 1) for h in (0, 1)]
     for flow in flows:
         to_mate(mate, *flow).wait_recv()
         for j in range(1, n_y):
             pass_on(y_source(j) + 1 - core, *flow, j).wait_recv()
-    to_expert(1, half - 1).wait_send()
-    for far, r in flows:
-        if not far and r:
-            to_expert(far, r).wait_send()
-        to_mate(d, far, r).wait_send()
+    to_expert(*far_flows[-2]).wait_send()
+    to_expert(*far_flows[-1]).wait_send()
+    for flow in near_flows:
+        to_expert(*flow).wait_send()
+    for flow in flows:
+        to_mate(d, *flow).wait_send()
         for j in range(1, n_y):
-            to_y(d, far, r, j).wait_send()
-            pass_on(y_source(j) + core, far, r, j).wait_send()
+            to_y(d, *flow, j).wait_send()
+            pass_on(y_source(j) + core, *flow, j).wait_send()
 
 
 def dispatch(send, n_dp, n_ex):
@@ -127,10 +138,7 @@
         out_shape=jax.ShapeDtypeStruct((n_dp, n_ex, rows, width), send.dtype),
         in_specs=[pl.BlockSpec(memory_space=pl.ANY)],
         out_specs=pl.BlockSpec(memory_space=pl.ANY),
-        scratch_shapes=[
-            dma, dma((2, half)), dma((2, half)), dma((2, half)), dma((2, half)),
-            dma((n_y, 2, half)), dma((n_y, 2, half)), dma((n_y, 2, half)), dma((n_y, 2, half)),
-        ],
+        scratch_shapes=[dma] + [dma((2, half, 2))] * 4 + [dma((n_y, 2, half, 2))] * 4,
         compiler_params=pltpu.CompilerParams(collective_id=0, has_side_effects=True),
     )(send)
 
@@ -191,11 +199,12 @@
         jnp.dot(left, flat_weights[: 2 * hid, :half], preferred_element_type=F32)
         + jnp.dot(right, flat_weights[: 2 * hid, half:], preferred_element_type=F32)
     ).astype(BF16)
+    all_route = lax.all_gather(route_rows, "expert", axis=0, tiled=False)
+    all_route, input_rows, rows = lax.optimization_barrier((all_route, input_rows, rows))
+    back_route = lax.dynamic_index_in_dim(all_route, lax.axis_index("expert"), 1, keepdims=False)
     back = lax.all_to_all(
         input_rows.reshape(n_ex, slab, half), "expert", split_axis=0, concat_axis=0, tiled=True
     )
-    all_route = lax.all_gather(route_rows, "expert", axis=0, tiled=False)
-    back_route = lax.dynamic_index_in_dim(all_route, lax.axis_index("expert"), 1, keepdims=False)
 
     own_weights = lax.dynamic_slice_in_dim(weights, d * part, part, axis=1).reshape(3 * part, width)
     every = rows.reshape(n_dp * n_ex * slab, width)

time: 285 us -> 267 us (0.937)
  blocking collectives: 41.8 us -> 31.1 us
  Pallas kernels: 139 us -> 132 us
    all_gather x1, blocking collectives: 41.8 us -> 31.1 us  [shards(): all_route = lax.all_gather(route_rows, 'expert', axis=0, tiled=False)]
    pallas_call x1, Pallas kernels: 139 us -> 132 us  [dispatch(): pl.pallas_call(functools.partial(dispatch_kernel, n_dp, n_ex), out_shape=...]
  transfers between devices with their start and end apart: 1 -> 1, of which waited for: 0 -> 0; matrix products, arithmetic and copies ran while one was open for 18% -> 19% of each run, Pallas kernels for 0% -> 0%
where the time goes in v3:
time: 267 us
  Pallas kernels  132 us (49%)
  matrix products  76.9 us (29%)
  blocking collectives  31.1 us (12%)
  other arithmetic  12.3 us (5%)
  local copies, waits for them, and re-layouts  8.21 us (3%)
  starting transfers between devices  5.98 us (2%)
    pallas_call x1, Pallas kernels, dispatch(): pl.pallas_call(functools.partial(dispatch_kernel, n_dp, n_ex), out_shape=...  132 us
    all_gather x1, blocking collectives, shards(): all_route = lax.all_gather(route_rows, 'expert', axis=0, tiled=False)  31.1 us
    dot_general x1, matrix products, shards(): lax.dot_general(every, own_weights, (((1,), (1,)), ((), ())), preferred_e...  19 us
    dot_general x1, matrix products, shards(): lax.dot_general(mine, flat_weights, (((1,), (1,)), ((), ())), preferred_e...  16.9 us
    dot_general x1, matrix products, shards(): lax.dot_general(factors, every, (((0,), (0,)), ((), ())), preferred_eleme...  16.8 us
    dot_general x1, matrix products, shards(): jnp.dot(left, flat_weights[:2 * hid, :half], preferred_element_type=F32)  7.84 us
    all_to_all x1, starting transfers between devices, shards(): lax.all_to_all(input_rows.reshape(n_ex, slab, half), 'expert', split_axis...  5.98 us
    dot_general x1, matrix products, shards(): jnp.dot(right, flat_weights[:2 * hid, half:], preferred_element_type=F32)  5.84 us
  transfers between devices with their start and end apart: 1, of which 0 were waited for; matrix products, arithmetic and copies ran while one was open for 19% of the time, Pallas kernels for 0%

profile of v3, /device:TPU:0, one launch (start us, length us, event | category | flops | bytes accessed | tf_op | source)
XLA Modules:
  0.0 267.0 jit_solution(11021541838611015532)
XLA Ops:
  0.8 0.8 fusion.20
  2.0 0.7 convert_convert_fusion
  2.7 0.7 select_reduce_fusion.3
  3.8 0.4 fusion.16
  4.2 1.4 fusion.24
  5.6 3.8 %add_convert_fusion = bf16[576,4096]{1,0:T(8,128)(2,1)} fusion(f32[576,4096]{1,0:T(8,128)S(1)} %fusion.24, pred[576,192]{1,0:T(32,128)(4,1)S(1)} %get-tuple-element.17, bf16[192,4096]{1,0:T(8,128)(2,1)S(1)} %copy-done.2, f32[576]{0:T(1024)S(1)} %mul.64), kind=kOutput, calls=%fused_computation | convolution fusion | flops 913047552 | bytes 15841536 | tf_op jit(solution)/shard_map/dot_general | solution.py:181
  9.4 131.6 %shard_map.76 = bf16[4,8,72,4096]{3,2,1,0:T(8,128)(2,1)} custom-call(bf16[8,72,4096]{2,1,0:T(8,128)(2,1)} %bitcast.68), custom_call_target="tpu_custom_call" | custom-call | tf_op jit(solution)/shard_map/pallas_call | solution.py:136
  141.0 16.9 %fusion.5 = f32[8,72,2112]{2,1,0:T(8,128)S(1)} fusion(bf16[2112,4096,1]{1,0,2:T(8,128)(2,1)} %bitcast.77, bf16[4,8,72,4096]{3,2,1,0:T(8,128)(2,1)} %shard_map.76, s32[]{:T(128)S(6)} %select_n.35), kind=kOutput, calls=%fused_computation.8 | convolution fusion | flops 9965666304 | bytes 26886148 | tf_op jit(solution)/shard_map/dot_general | solution.py:190
  157.9 0.8 multiply_convert_fusion.4
  158.7 31.1 %all-gather = f32[64,36]{1,0:T(8,128)S(1)} all-gather(f32[8,36]{1,0:T(8,128)S(1)} %get-tuple-element.13), channel_id=2, replica_groups=mesh['dp'=4,'expert'=8] {'expert'}, dimensions={0}, use_global_device_ids=true | all-gather | bytes 10368 | tf_op jit(solution)/shard_map/all_gather | solution.py:202
  190.1 0.4 fusion.23
  190.5 5.8 %fusion.1 = f32[576,2048]{1,0:T(8,128)S(1)} fusion(bf16[576,1408]{1,0:T(8,128)(2,1)S(1)} %bitcast.76, bf16[2112,4096]{1,0:T(8,128)(2,1)} %bitcast.78), kind=kOutput, calls=%fused_computation.4 | convolution fusion | flops 3321888768 | bytes 12107776 | tf_op jit(solution)/shard_map/dot_general | solution.py:200
  196.4 7.8 %add_convert_fusion.1 = bf16[576,2048]{1,0:T(8,128)(2,1)} fusion(f32[576,2048]{1,0:T(8,128)S(1)} %fusion.1, bf16[576,1408]{1,0:T(8,128)(2,1)S(1)} %bitcast.75, bf16[2112,4096]{1,0:T(8,128)(2,1)} %bitcast.79), kind=kOutput, calls=%fused_computation.10 | convolution fusion | flops 3324248064 | bytes 14467072 | tf_op jit(solution)/shard_map/dot_general | solution.py:199
  204.2 6.0 %all-to-all-start = ((bf16[8,72,2048]{2,1,0:T(8,128)(2,1)}), bf16[8,72,2048]{2,1,0:T(8,128)(2,1)}, u32[]{:S(2)}, u32[]{:S(2)}) async-start(bf16[8,72,2048]{2,1,0:T(8,128)(2,1)} %bitcast.74), calls=%async_computation | async-start | bytes 4718592 | tf_op jit(solution)/shard_map/all_to_all | solution.py:205
  210.2 2.7 %constant_dynamic-slice_fusion = bf16[1,176,3,4096]{3,1,2,0:T(8,128)(2,1)S(1)} fusion(bf16[1,704,3,4096]{3,1,2,0:T(8,128)(2,1)} %param.9, s32[]{:T(128)S(6)} %select_n.39), kind=kLoop, calls=%fused_computation.49 | loop fusion | bytes 8650756 | tf_op jit(solution)/shard_map/dynamic-slice.1
  212.9 19.0 %fusion.25 = f32[32,72,528]{2,1,0:T(8,128)} fusion(bf16[32,72,4096]{2,1,0:T(8,128)(2,1)} %bitcast.69, bf16[528,4096,1]{1,0,2:T(8,128)(2,1)S(1)} %bitcast.72), kind=kOutput, calls=%fused_computation.57 | convolution fusion | flops 9965666304 | bytes 28065792 | tf_op jit(solution)/shard_map/dot_general | solution.py:211
  232.1 3.5 %multiply_convert_fusion.2 = (bf16[32,36,176]{2,1,0:T(8,128)(2,1)S(1)}, bf16[32,36,176]{2,1,0:T(8,128)(2,1)S(1)}, bf16[32,36,176]{2,1,0:T(8,128)(2,1)S(1)}) fusion(f32[32,72,528]{2,1,0:T(8,128)} %fusion.25), kind=kLoop, calls=%fused_computation.20 | loop fusion | flops 3244032 | bytes 3649536 | tf_op jit(solution)/shard_map/convert_element_type | solution.py:151
  235.5 2.7 %fusion.10 = bf16[32,72,528]{2,1,0:T(8,128)(2,1)} fusion(bf16[32,36,176]{2,1,0:T(8,128)(2,1)S(1)} %get-tuple-element.10, bf16[32,36,176]{2,1,0:T(8,128)(2,1)S(1)} %get-tuple-element.11, bf16[32,36,176]{2,1,0:T(8,128)(2,1)S(1)} %get-tuple-element.9, bf16[72,528]{1,0:T(8,128)(2,1)S(1)} %pad.5.clone), kind=kLoop, calls=%fused_computation.12 | loop fusion | flops 12165120 | bytes 3725568 | tf_op jit(solution)/shard_map/concatenate | solution.py:216
  238.2 4.5 %copy.18 = bf16[528,2304]{1,0:T(8,128)(2,1)} copy(bf16[528,2304]{0,1:T(8,128)(2,1)} %bitcast.71) | data formatting | bytes 4866048 | tf_op jit(solution)/shard_map/dot_general | solution.py:217
  243.1 0.6 divide_convert_fusion
  243.7 16.8 %convolution_bitcast_fusion = f32[1,176,3,4096]{3,1,2,0:T(8,128)} fusion(bf16[3,176,2304]{2,1,0:T(8,128)(2,1)} %bitcast.73, bf16[2304,4096,1]{1,0,2:T(8,128)(2,1)} %bitcast.70), kind=kOutput, calls=%fused_computation.1 | convolution fusion | flops 9965666304 | bytes 29958144 | tf_op jit(solution)/shard_map/dot_general | solution.py:217
  260.5 2.7 %fusion.12 = bf16[192,2048]{1,0:T(8,128)(2,1)S(1)} fusion(bf16[8,72,2048]{2,1,0:T(8,128)(2,1)} %all-to-all-done, s32[8,192]{1,0:T(8,128)S(1)} %fusion.13, s32[72]{0:T(128)S(1)} %iota_add_fusion, pred[72]{0:T(512)(128)(4,1)S(1)} %iota_compare_fusion.5), kind=kOutput, calls=%fused_computation.16 | convolution fusion | flops 453599232 | bytes 3152232 | tf_op jit(solution)/shard_map/dot_general | solution.py:223
  263.2 2.6 fusion.11
  265.7 1.3 pad_maximum_fusion
  (32 shorter events, 1.6 us)
Async XLA Ops:
  0.6 3.6 %copy-start = (bf16[192,4096]{1,0:T(8,128)(2,1)S(1)}, bf16[192,4096]{1,0:T(8,128)(2,1)}, u32[]{:S(2)}) copy-start(bf16[192,4096]{1,0:T(8,128)(2,1)} %param.5) | copy-start | bytes 4718596
  4.2 1.4 copy-start.2
  204.2 56.3 %all-to-all-start = ((bf16[8,72,2048]{2,1,0:T(8,128)(2,1)}), bf16[8,72,2048]{2,1,0:T(8,128)(2,1)}, u32[]{:S(2)}, u32[]{:S(2)}) async-start(bf16[8,72,2048]{2,1,0:T(8,128)(2,1)} %bitcast.74), calls=%async_computation | async-start | bytes 4718592 | tf_op jit(solution)/shard_map/all_to_all | solution.py:205
  238.2 4.8 %copy-start.3 = (s32[192,6]{0,1:T(8,128)S(1)}, s32[192,6]{0,1:T(8,128)}, u32[]{:S(2)}) copy-start(s32[192,6]{0,1:T(8,128)} %param.7) | copy-start | bytes 13828
  238.2 4.9 %copy-start.4 = (f32[192,6]{0,1:T(8,128)S(1)}, f32[192,6]{0,1:T(8,128)}, u32[]{:S(2)}) copy-start(f32[192,6]{0,1:T(8,128)} %param.8) | copy-start | bytes 13828
  260.5 6.5 %copy-start.1 = (bf16[192,4096]{1,0:T(8,128)(2,1)S(1)}, bf16[192,4096]{1,0:T(8,128)(2,1)}, u32[]{:S(2)}) copy-start(bf16[192,4096]{1,0:T(8,128)(2,1)} %param.5) | copy-start | bytes 4718596
